TPU v7x, 128 devices: a whole 4x4x4 slice. The times are simulated.
128 devices in a mesh: seq: 4 (over x), fsdp: 32 (over z, y, core).
Axes of the slice: x: 4, y: 4, z: 4, core: 2. Of those that a mesh axis runs over, the one named last changes fastest.
Arguments:
- hidden: bfloat16 [32, 1536, 768], P('fsdp', 'seq'), may hold values from -6 to 6
- lengths: int32 [32, 4], P('fsdp'), may hold values from 1 to 1344, 1536 in all within a row
- attn_gain: bfloat16 [768], P('fsdp'), may hold values from 0.5 to 1.5
- w_qkv: bfloat16 [768, 2304], P('fsdp'), may hold values from -0.21875 to 0.21875
- w_attn_out: bfloat16 [768, 768], P('fsdp'), may hold values from -1.75 to 1.75
- mlp_gain: bfloat16 [768], P('fsdp'), may hold values from 0.5 to 1.5
- w_in: bfloat16 [768, 2304], P('fsdp'), may hold values from -0.21875 to 0.21875
- w_mlp_out: bfloat16 [1152, 768], P('fsdp'), may hold values from -0.1875 to 0.1875
- cotangent: bfloat16 [32, 1536, 768], P('fsdp', 'seq'), may hold values from -6 to 6
Outputs:
- output: bfloat16 [32, 1536, 768], P('fsdp', 'seq')
- input_grad: float32 [32, 1536, 768], P('fsdp', 'seq')
- grad_attn_gain: float32 [768], P('fsdp')
- grad_qkv_weight: float32 [768, 2304], P('fsdp', 'seq')
- grad_attn_out: float32 [768, 768], P('fsdp', 'seq')
- grad_mlp_gain: float32 [768], P('fsdp')
- grad_w_in: float32 [768, 2304], P('fsdp', 'seq')
- grad_mlp_out: float32 [1152, 768], P('fsdp', 'seq')
Inputs may be any that keep to these rules, and one draw needn't show every extreme that they name: `lengths`: each row sums to 1536; its largest entry is exactly 1344.
All inputs are finite; a program needn't handle non-finite values.
Results may differ from a plain program's by a relative error of at most 0.017.
Values may be sent and summed in bfloat16 or wider, within the bound.
A program may use at most 128 MiB of HBM per device.

v0:
```python
import math

import jax
import jax.numpy as jnp
from jax import lax
from jax.sharding import PartitionSpec as P

HEADS = 12
HEAD_DIM = 64


def norm_stats(values):
    average = jnp.mean(values, axis=-1, keepdims=True)
    centred = values - average
    variance = jnp.mean(centred * centred, axis=-1, keepdims=True)
    return centred * lax.rsqrt(variance + 1e-05)


def gained_norm(values, gain):
    return norm_stats(values) * gain


def gated(inner, gate):
    return jax.nn.gelu(inner, approximate=False) * gate


def doc_tables(lengths, places, head_dim):
    doc_ends = jnp.cumsum(lengths)
    starts = doc_ends - lengths
    member = (places[:, None] >= starts[None, :]) & (places[:, None] < doc_ends[None, :])
    numbers = jnp.arange(lengths.shape[0], dtype=jnp.int32)
    segment = jnp.sum(jnp.where(member, numbers[None, :], 0), axis=1)
    offset = jnp.sum(jnp.where(member, starts[None, :], 0), axis=1)
    position = (places - offset).astype(jnp.float32)
    halfway = head_dim // 2
    inverse = jnp.exp(
        jnp.arange(halfway, dtype=jnp.float32) * (-2.0 * math.log(160000.0) / head_dim)
    )
    angles = position[:, None] * inverse[None, :]
    angles = jnp.concatenate([angles, angles], axis=-1)
    return (segment, jnp.cos(angles), jnp.sin(angles))


def rotate(values, cosine, sine_table):
    halfway = values.shape[-1] // 2
    turned = jnp.concatenate([-values[..., halfway:], values[..., :halfway]], axis=-1)
    return values * cosine[:, None, :] + turned * sine_table[:, None, :]


def unrotate(grad_rows, cosine, sine_table):
    halfway = grad_rows.shape[-1] // 2
    scaled = grad_rows * sine_table[:, None, :]
    turned = jnp.concatenate([scaled[..., halfway:], -scaled[..., :halfway]], axis=-1)
    return grad_rows * cosine[:, None, :] + turned


def times_t(left, right):
    return lax.dot_general(
        left, right, (((1,), (1,)), ((), ())), preferred_element_type=jnp.float32
    )


def outer_sum(left, right):
    return lax.dot_general(
        left, right, (((0,), (0,)), ((), ())), preferred_element_type=jnp.float32
    )


def block_scores(query_block, key_head, seg_block, segment, score_scale):
    scores = times_t(query_block, key_head) * score_scale
    return jnp.where(seg_block[:, None] == segment[None, :], scores, -1000000000.0)


def head_forward(query_head, key_head, value_head, segment, block_rows):
    block_count = query_head.shape[0] // block_rows
    score_scale = query_head.shape[-1] ** (-0.5)

    def one_block(block_index):
        query_block = lax.dynamic_slice_in_dim(query_head, block_index * block_rows, block_rows, 0)
        seg_block = lax.dynamic_slice_in_dim(segment, block_index * block_rows, block_rows, 0)
        scores = block_scores(query_block, key_head, seg_block, segment, score_scale)
        highest = jnp.max(scores, axis=-1, keepdims=True)
        weights = jnp.exp(scores - highest)
        totals = jnp.sum(weights, axis=-1, keepdims=True)
        shares = (weights / totals).astype(jnp.bfloat16)
        mixture = jnp.dot(shares, value_head, preferred_element_type=jnp.float32).astype(
            jnp.bfloat16
        )
        return (mixture, (highest + jnp.log(totals))[:, 0])

    mixture, logsum = lax.map(one_block, jnp.arange(block_count, dtype=jnp.int32))
    return (mixture.reshape(-1, value_head.shape[-1]), logsum.reshape(-1))


def head_backward(query_head, key_head, value_head, grad_head, logsum, segment, block_rows):
    block_count = query_head.shape[0] // block_rows
    score_scale = query_head.shape[-1] ** (-0.5)

    def one_block(carried, block_index):
        key_grad, value_grad = carried
        first = block_index * block_rows
        query_block = lax.dynamic_slice_in_dim(query_head, first, block_rows, 0)
        grad_block = lax.dynamic_slice_in_dim(grad_head, first, block_rows, 0)
        seg_block = lax.dynamic_slice_in_dim(segment, first, block_rows, 0)
        sum_block = lax.dynamic_slice_in_dim(logsum, first, block_rows, 0)
        scores = block_scores(query_block, key_head, seg_block, segment, score_scale)
        shares = jnp.exp(scores - sum_block[:, None])
        share_low = shares.astype(jnp.bfloat16)
        grad_shares = times_t(grad_block, value_head)
        inner = jnp.sum(grad_shares * shares, axis=-1, keepdims=True)
        grad_scores = (shares * (grad_shares - inner)).astype(jnp.bfloat16)
        query_grad = (
            jnp.dot(grad_scores, key_head, preferred_element_type=jnp.float32) * score_scale
        ).astype(jnp.bfloat16)
        key_grad = key_grad + outer_sum(grad_scores, query_block) * score_scale
        value_grad = value_grad + outer_sum(share_low, grad_block)
        return ((key_grad, value_grad), query_grad)

    zeros = jnp.zeros(key_head.shape, jnp.float32)
    (key_grad, value_grad), query_grad = lax.scan(
        one_block, (zeros, zeros), jnp.arange(block_count, dtype=jnp.int32)
    )
    return (
        query_grad.reshape(-1, key_head.shape[-1]),
        key_grad.astype(jnp.bfloat16),
        value_grad.astype(jnp.bfloat16),
    )


def sum_rows(parts):
    return (
        lax.psum_scatter(parts[0], "fsdp", scatter_dimension=0, tiled=True),
        lax.psum_scatter(parts[1], "fsdp", scatter_dimension=0, tiled=True),
        lax.psum_scatter(parts[2], "fsdp", scatter_dimension=0, tiled=True),
        lax.psum_scatter(parts[3], "fsdp", scatter_dimension=0, tiled=True),
        lax.psum_scatter(parts[4], "fsdp", scatter_dimension=0, tiled=True),
        lax.psum_scatter(parts[5], "fsdp", scatter_dimension=0, tiled=True),
    )


def sum_cols(parts):
    return (
        lax.psum_scatter(
            parts[0].astype(jnp.bfloat16), "seq", scatter_dimension=1, tiled=True
        ).astype(jnp.float32),
        lax.psum_scatter(
            parts[1].astype(jnp.bfloat16), "seq", scatter_dimension=1, tiled=True
        ).astype(jnp.float32),
        lax.psum_scatter(
            parts[2].astype(jnp.bfloat16), "seq", scatter_dimension=1, tiled=True
        ).astype(jnp.float32),
        lax.psum_scatter(
            parts[3].astype(jnp.bfloat16), "seq", scatter_dimension=1, tiled=True
        ).astype(jnp.float32),
    )


def sum_gains(parts):
    return lax.psum((parts[0], parts[1]), "seq")


def body(hidden, lengths, attn_gain, w_qkv, w_attn_out, mlp_gain, w_in, w_mlp_out, cotangent):
    seq_count = lax.axis_size("seq")
    rank = lax.axis_index("seq")
    tokens = hidden.shape[1]
    width = hidden.shape[2]
    pack = tokens * seq_count
    local_heads = HEADS // seq_count
    block_rows = min(512, pack)
    gain_one, weight_qkv, weight_out = (
        lax.all_gather(attn_gain, "fsdp", axis=0, tiled=True),
        lax.all_gather(w_qkv, "fsdp", axis=0, tiled=True),
        lax.all_gather(w_attn_out, "fsdp", axis=0, tiled=True),
    )
    gain_two, weight_in, weight_down = (
        lax.all_gather(mlp_gain, "fsdp", axis=0, tiled=True),
        lax.all_gather(w_in, "fsdp", axis=0, tiled=True),
        lax.all_gather(w_mlp_out, "fsdp", axis=0, tiled=True),
    )
    doc_lengths = lengths[0]
    places = rank * tokens + jnp.arange(tokens, dtype=jnp.int32)
    tables = doc_tables(doc_lengths, places, HEAD_DIM)
    cosine = tables[1]
    sine_table = tables[2]
    segment = doc_tables(doc_lengths, jnp.arange(pack, dtype=jnp.int32), HEAD_DIM)[0]
    inputs = hidden[0].astype(jnp.float32)
    gain_first = gain_one.astype(jnp.float32)
    attn_in = gained_norm(inputs, gain_first).astype(jnp.bfloat16)
    projected_qkv = jnp.dot(attn_in, weight_qkv, preferred_element_type=jnp.float32)
    query_rot = rotate(
        projected_qkv[:, :width].reshape(tokens, HEADS, HEAD_DIM), cosine, sine_table
    ).reshape(tokens, width)
    key_rot = rotate(
        projected_qkv[:, width : 2 * width].reshape(tokens, HEADS, HEAD_DIM), cosine, sine_table
    ).reshape(tokens, width)
    stacked = jnp.stack([query_rot, key_rot, projected_qkv[:, 2 * width :]]).astype(jnp.bfloat16)
    by_heads = lax.all_to_all(stacked, "seq", split_axis=2, concat_axis=1, tiled=True)
    head_major = by_heads.reshape(3, pack, local_heads, HEAD_DIM).transpose(0, 2, 1, 3)

    def run_forward(parts):
        return head_forward(parts[0], parts[1], parts[2], segment, block_rows)

    mixture, logsum = lax.map(run_forward, (head_major[0], head_major[1], head_major[2]))
    merged = mixture.transpose(1, 0, 2).reshape(pack, local_heads * HEAD_DIM)
    attn_tok = lax.all_to_all(merged, "seq", split_axis=0, concat_axis=1, tiled=True)
    residual = inputs + jnp.dot(attn_tok, weight_out, preferred_element_type=jnp.float32)
    gain_second = gain_two.astype(jnp.float32)
    mlp_in = gained_norm(residual, gain_second).astype(jnp.bfloat16)
    projected = jnp.dot(mlp_in, weight_in, preferred_element_type=jnp.float32)
    ff_width = weight_down.shape[0]
    activated = gated(projected[:, :ff_width], projected[:, ff_width:]).astype(jnp.bfloat16)
    output = residual + jnp.dot(activated, weight_down, preferred_element_type=jnp.float32)
    grad_output = cotangent[0].astype(jnp.float32)
    grad_branch = grad_output.astype(jnp.bfloat16)
    grad_down = outer_sum(activated, grad_branch)
    grad_act = times_t(grad_branch, weight_down)
    gate_pullback = jax.vjp(gated, projected[:, :ff_width], projected[:, ff_width:])[1]
    grad_inner, grad_gate = gate_pullback(grad_act)
    grad_proj = jnp.concatenate([grad_inner, grad_gate], axis=1).astype(jnp.bfloat16)
    grad_in = outer_sum(mlp_in, grad_proj)
    grad_norm_two = times_t(grad_proj, weight_in)
    grad_resid_ln, grad_gain_two = jax.vjp(gained_norm, residual, gain_second)[1](grad_norm_two)
    grad_resid = grad_output + grad_resid_ln
    grad_attn = grad_resid.astype(jnp.bfloat16)
    grad_out = outer_sum(attn_tok, grad_attn)
    grad_mixed = times_t(grad_attn, weight_out).astype(jnp.bfloat16)
    grad_heads = lax.all_to_all(grad_mixed, "seq", split_axis=1, concat_axis=0, tiled=True)
    grad_major = grad_heads.reshape(pack, local_heads, HEAD_DIM).transpose(1, 0, 2)

    def run_backward(parts):
        return head_backward(parts[0], parts[1], parts[2], parts[3], parts[4], segment, block_rows)

    query_grad, key_grad, value_grad = lax.map(
        run_backward, (head_major[0], head_major[1], head_major[2], grad_major, logsum)
    )
    stacked_grad = (
        jnp.stack([query_grad, key_grad, value_grad])
        .transpose(0, 2, 1, 3)
        .reshape(3, pack, local_heads * HEAD_DIM)
    )
    back_tok = lax.all_to_all(stacked_grad, "seq", split_axis=1, concat_axis=2, tiled=True)
    grad_query = unrotate(
        back_tok[0].astype(jnp.float32).reshape(tokens, HEADS, HEAD_DIM), cosine, sine_table
    ).reshape(tokens, width)
    grad_key = unrotate(
        back_tok[1].astype(jnp.float32).reshape(tokens, HEADS, HEAD_DIM), cosine, sine_table
    ).reshape(tokens, width)
    grad_qkv = jnp.concatenate(
        [grad_query, grad_key, back_tok[2].astype(jnp.float32)], axis=1
    ).astype(jnp.bfloat16)
    grad_wqkv = outer_sum(attn_in, grad_qkv)
    grad_norm_one = times_t(grad_qkv, weight_qkv)
    grad_input_ln, grad_gain_one = jax.vjp(gained_norm, inputs, gain_first)[1](grad_norm_one)
    input_grad = grad_resid + grad_input_ln
    rows = sum_rows((grad_gain_one, grad_wqkv, grad_out, grad_gain_two, grad_in, grad_down))
    matrices = sum_cols((rows[1], rows[2], rows[4], rows[5]))
    gains = sum_gains((rows[0], rows[3]))
    return (
        output.astype(jnp.bfloat16)[None],
        input_grad[None],
        gains[0],
        matrices[0],
        matrices[1],
        gains[1],
        matrices[2],
        matrices[3],
    )


def solution(mesh):
    in_specs = (
        P("fsdp", "seq", None),
        P("fsdp", None),
        P("fsdp"),
        P("fsdp", None),
        P("fsdp", None),
        P("fsdp"),
        P("fsdp", None),
        P("fsdp", None),
        P("fsdp", "seq", None),
    )
    out_specs = (
        P("fsdp", "seq", None),
        P("fsdp", "seq", None),
        P("fsdp"),
        P("fsdp", "seq"),
        P("fsdp", "seq"),
        P("fsdp"),
        P("fsdp", "seq"),
        P("fsdp", "seq"),
    )
    return jax.shard_map(body, mesh=mesh, in_specs=in_specs, out_specs=out_specs, check_vma=False)
```

profile of v0, /device:TPU:0, one launch (start us, length us, event | category | flops | bytes accessed | tf_op | source)
XLA Modules:
  0.0 764.0 jit_solution(6573693328931216630)
XLA Ops:
  13.2 69.5 %all-reduce.8 = (bf16[768]{0:T(1024)(128)(2,1)S(1)}, bf16[768]{0:T(1024)(128)(2,1)}) all-reduce(bf16[768]{0:T(1024)(128)(2,1)S(1)} %dynamic-update-slice, bf16[768]{0:T(1024)(128)(2,1)S(1)} %dynamic-update-slice.1), channel_id=1, replica_groups=mesh['seq'=4,'fsdp'=32] {'fsdp'}, use_global_device_ids=true, to_apply=%add | all-reduce | flops 1536 | bytes 6144
  90.6 3.6 fusion.72
  111.7 4.2 all-to-all-start
  117.2 23.6 %all-to-all-done = bf16[3,384,768]{1,0,2:T(4,128)(2,1)S(1)} async-done(((bf16[3,384,768]{1,0,2:T(4,128)(2,1)}), bf16[3,384,768]{1,0,2:T(4,128)(2,1)S(1)}, u32[]{:S(2)}, u32[]{:S(2)}) %all-to-all-start) | async-done | bytes 1769504 | tf_op jit(solution)/shard_map/all_to_all | solution.py:197
  147.4 85.4 %while.54 = (s32[]{:T(128)}, bf16[3,1536,64]{2,1,0:T(8,128)(2,1)}, f32[3,1536]{1,0:T(4,128)}, bf16[3,1536,64]{2,1,0:T(8,128)(2,1)}, bf16[3,1536,64]{2,1,0:T(8,12...) while((s32[]{:T(128)}, bf16[3,1536,64]{2,1,0:T(8,128)(2,1)}, ...), condition=%wide.region_10.11_spmd, body=%wide.region_5.10_spmd.sunk | while | flops 208436736 | bytes 12447160 | solution.py:203
  151.2 20.7 %while.57 = (s32[]{:T(128)}, bf16[3,512,64]{1,2,0:T(8,128)(2,1)}, f32[3,512]{1,0:T(4,128)}, s32[3]{0:T(128)S(1)}, s32[1536]{0:T(1024)}, /*index=5*/bf16[1536,64]...) while((s32[]{:T(128)}, bf16[3,512,64]{1,2,0:T(8,128)(2,1)}, ...), condition=%wide.region_9.9_spmd, body=%wide.region_6.8_spmd.sunk | while | flops 208436736 | bytes 10259131 | solution.py:91
  179.6 20.7 %while.57 = (s32[]{:T(128)}, bf16[3,512,64]{1,2,0:T(8,128)(2,1)}, f32[3,512]{1,0:T(4,128)}, s32[3]{0:T(128)S(1)}, s32[1536]{0:T(1024)}, /*index=5*/bf16[1536,64]...) while((s32[]{:T(128)}, bf16[3,512,64]{1,2,0:T(8,128)(2,1)}, ...), condition=%wide.region_9.9_spmd, body=%wide.region_6.8_spmd.sunk | while | flops 208436736 | bytes 10259131 | solution.py:91
  208.1 20.7 %while.57 = (s32[]{:T(128)}, bf16[3,512,64]{1,2,0:T(8,128)(2,1)}, f32[3,512]{1,0:T(4,128)}, s32[3]{0:T(128)S(1)}, s32[1536]{0:T(1024)}, /*index=5*/bf16[1536,64]...) while((s32[]{:T(128)}, bf16[3,512,64]{1,2,0:T(8,128)(2,1)}, ...), condition=%wide.region_9.9_spmd, body=%wide.region_6.8_spmd.sunk | while | flops 208436736 | bytes 10259131 | solution.py:91
  235.4 3.5 all-to-all-start.1
  239.8 3.7 reshape.290
  243.5 3.8 all-to-all-done.1
  249.9 3.8 fusion.75
  253.7 5.8 add_convert_fusion
  262.9 78.3 %fusion = f32[40,768]{1,0:T(8,128)} fusion(f32[1152,768]{1,0:T(8,128)S(1)} %fusion.57), kind=kCustom, calls=%all-reduce-scatter | all-reduce-scatter fusion | flops 983041 | bytes 3662336
  347.9 5.3 multiply_reduce_fusion.1
  363.8 3.5 all-to-all-start.2
  367.6 5.0 fusion.49
  372.7 3.8 all-to-all-done.2
  378.0 156.1 %while.56 = (s32[]{:T(128)}, bf16[3,1536,64]{1,2,0:T(8,128)(2,1)}, bf16[3,1536,64]{1,2,0:T(8,128)(2,1)}, bf16[3,1536,64]{1,2,0:T(8,128)(2,1)}, bf16[3,1536,64]{2...) while((s32[]{:T(128)}, bf16[3,1536,64]{1,2,0:T(8,128)(2,1)}, ...), condition=%wide.region_19.20_spmd, body=%wide.region_15.19_spmd.sunk | while | flops 511933952 | bytes 39557740 | solution.py:233
  384.5 41.0 %while.58 = (s32[]{:T(128)}, f32[1536,64]{0,1:T(8,128)}, f32[1536,64]{0,1:T(8,128)}, bf16[3,512,64]{1,2,0:T(8,128)(2,1)}, s32[3]{0:T(128)S(1)}, /*index=5*/s32[1...) while((s32[]{:T(128)}, f32[1536,64]{0,1:T(8,128)}, ...), condition=%wide.region_18.18_spmd.clone, body=%wide.region_16.17_spmd.clone.sunk | while | flops 511737344 | bytes 33645344 | solution.py:120
  436.4 41.0 %while.58 = (s32[]{:T(128)}, f32[1536,64]{0,1:T(8,128)}, f32[1536,64]{0,1:T(8,128)}, bf16[3,512,64]{1,2,0:T(8,128)(2,1)}, s32[3]{0:T(128)S(1)}, /*index=5*/s32[1...) while((s32[]{:T(128)}, f32[1536,64]{0,1:T(8,128)}, ...), condition=%wide.region_18.18_spmd.clone, body=%wide.region_16.17_spmd.clone.sunk | while | flops 511737344 | bytes 33645344 | solution.py:120
  488.4 41.2 %while.58 = (s32[]{:T(128)}, f32[1536,64]{0,1:T(8,128)}, f32[1536,64]{0,1:T(8,128)}, bf16[3,512,64]{1,2,0:T(8,128)(2,1)}, s32[3]{0:T(128)S(1)}, /*index=5*/s32[1...) while((s32[]{:T(128)}, f32[1536,64]{0,1:T(8,128)}, ...), condition=%wide.region_18.18_spmd.clone, body=%wide.region_16.17_spmd.clone.sunk | while | flops 511737344 | bytes 33645344 | solution.py:120
  537.0 4.1 copy.172
  541.1 36.9 %all_to_all.65 = bf16[3,1536,192]{2,0,1:T(4,128)(2,1)} all-to-all(bf16[3,1536,192]{2,0,1:T(4,128)(2,1)S(1)} %copy.172), channel_id=1, replica_groups=mesh['seq'=4,'fsdp'=32] {'seq'}, dimensions={1} | all-to-all | bytes 3538944 | tf_op jit(solution)/shard_map/all_to_all | solution.py:241
  578.0 4.4 copy.174
  586.1 5.2 fusion.52
  597.5 4.3 fusion.46
  604.9 66.3 %all-reduce.6 = (f32[768]{0:T(1024)}, f32[768]{0:T(1024)}) all-reduce(f32[768]{0:T(1024)} %get-tuple-element.340, f32[768]{0:T(1024)} %get-tuple-element.338), channel_id=2, replica_groups=mesh['seq'=4,'fsdp'=32] {'fsdp'}, use_global_device_ids=true, to_apply=%region_23.24.clone | all-reduce | flops 1536 | bytes 12288
  673.7 9.4 %all-reduce.7 = (f32[24]{0:T(128)}, f32[24]{0:T(128)}) all-reduce(f32[24]{0:T(128)} %dynamic-slice.3, f32[24]{0:T(128)} %dynamic-slice.5), channel_id=1, replica_groups=mesh['seq'=4,'fsdp'=32] {'seq'}, use_global_device_ids=true, to_apply=%region_24.25 | all-reduce | flops 48 | bytes 384 | tf_op jit(solution)/shard_map/psum | solution.py:159
  693.9 13.8 %reduce-scatter.26.cloned.1.call-done = bf16[192,24]{1,0:T(8,128)(2,1)} async-done(((bf16[768,24]{1,0:T(8,128)(2,1)}), bf16[192,24]{1,0:T(8,128)(2,1)}) %reduce-scatter.26.cloned.1.call-update) | async-done | bytes 9232
  709.1 22.3 %reduce-scatter.28.cloned.1.call-done = bf16[576,24]{1,0:T(8,128)(2,1)} async-done(((bf16[2304,24]{1,0:T(8,128)(2,1)}), bf16[576,24]{1,0:T(8,128)(2,1)}) %reduce-scatter.28.cloned.1.call-update) | async-done | bytes 27664
  733.0 22.3 %reduce-scatter.24.cloned.1.call-done = bf16[576,24]{1,0:T(8,128)(2,1)} async-done(((bf16[2304,24]{1,0:T(8,128)(2,1)}), bf16[576,24]{1,0:T(8,128)(2,1)}) %reduce-scatter.24.cloned.1.call-update) | async-done | bytes 27664
  (472 shorter events, 329.4 us)
Async XLA Ops:
  7.2 83.4 %all-gather.6.cloned.1.call-start = ((), (), s32[]{:S(2)}) async-start(), calls=%async_computation.11 | async-start | bytes 3649536 | tf_op jit(solution)/shard_map/all_gather | solution.py:172
  7.9 231.9 %all-gather.12.cloned.1.call-start = ((), (), s32[]{:S(2)}) async-start(), calls=%async_computation.17 | async-start | bytes 2027520 | tf_op jit(solution)/shard_map/all_gather | solution.py:178
  8.6 234.9 %all-gather.8.cloned.1.call-start = ((), (), s32[]{:S(2)}) async-start(), calls=%async_computation.12 | async-start | bytes 1216512 | tf_op jit(solution)/shard_map/all_gather | solution.py:173
  82.7 7.8 %copy-start.34 = (f32[768]{0:T(1024)}, f32[768]{0:T(1024)S(1)}, u32[]{:S(2)}) copy-start(f32[768]{0:T(1024)S(1)} %convert_element_type.121) | copy-start | bytes 9220
  84.0 6.6 copy-start.36
  85.9 4.6 copy-start.38
  99.3 5.6 copy-start.12
  111.7 29.1 %all-to-all-start = ((bf16[3,384,768]{1,0,2:T(4,128)(2,1)}), bf16[3,384,768]{1,0,2:T(4,128)(2,1)S(1)}, u32[]{:S(2)}, u32[]{:S(2)}) async-start(bf16[3,384,768]{1,0,2:T(4,128)(2,1)} %copy.155), calls=%async_computation | async-start | bytes 4718592 | tf_op jit(solution)/shard_map/all_to_all | solution.py:197
  115.9 133.9 %all-gather.10.cloned.1.call-start = ((), (), s32[]{:S(2)}) async-start(), calls=%async_computation.13 | async-start | bytes 3649536 | tf_op jit(solution)/shard_map/all_gather | solution.py:177
  234.4 4.7 copy-start.43
  235.4 11.9 %all-to-all-start.1 = ((bf16[4,384,192]{1,2,0:T(8,128)(2,1)}), bf16[4,384,192]{1,2,0:T(8,128)(2,1)S(1)}, u32[]{:S(2)}, u32[]{:S(2)}) async-start(bf16[4,384,192]{1,2,0:T(8,128)(2,1)} %copy.162), calls=%async_computation.1 | async-start | bytes 1179648 | tf_op jit(solution)/shard_map/all_to_all | solution.py:205
  238.9 357.1 %reduce-scatter.30.cloned.1.call-start = ((), (), s32[]{:S(2)}) async-start(), calls=%async_computation.21 | async-start | bytes 245760
  239.8 7.5 copy-start.4
  249.5 4.1 copy-start.6
  249.8 3.8 copy-start.15
  342.0 13.0 %collective-permute-start = (bf16[40,768]{1,0:T(8,128)(2,1)S(1)}, bf16[40,768]{1,0:T(8,128)(2,1)S(1)}, u32[]{:S(2)}, u32[]{:S(2)}) collective-permute-start(bf16[40,768]{1,0:T(8,128)(2,1)S(1)} %convert.75), channel_id=1, source_target_pairs={{0,1},{1,2},{2,3},{3,4},{4,5},{5,6},{6,7},{7,8},{8,9},{9,10},{10,1... | collective-permute-start | bytes 184328
  343.3 11.7 %collective-permute-start.1 = (bf16[40,768]{1,0:T(8,128)(2,1)S(1)}, bf16[40,768]{1,0:T(8,128)(2,1)S(1)}, u32[]{:S(2)}, u32[]{:S(2)}) collective-permute-start(bf16[40,768]{1,0:T(8,128)(2,1)S(1)} %convert.75), channel_id=1, source_target_pairs={{0,2},{1,3},{2,4},{3,5},{4,6},{5,7},{6,8},{7,9},{8,10},{9,11},{10,... | collective-permute-start | bytes 184328
  344.6 10.4 %collective-permute-start.2 = (bf16[40,768]{1,0:T(8,128)(2,1)S(1)}, bf16[40,768]{1,0:T(8,128)(2,1)S(1)}, u32[]{:S(2)}, u32[]{:S(2)}) collective-permute-start(bf16[40,768]{1,0:T(8,128)(2,1)S(1)} %convert.75), channel_id=1, source_target_pairs={{0,3},{1,4},{2,5},{3,6},{4,7},{5,8},{6,9},{7,10},{8,11},{9,12},{10... | collective-permute-start | bytes 184328
  346.6 8.3 %collective-permute-start.3 = (bf16[4,768]{1,0:T(4,128)(2,1)S(1)}, bf16[4,768]{1,0:T(4,128)(2,1)S(1)}, u32[]{:S(2)}, u32[]{:S(2)}) collective-permute-start(bf16[4,768]{1,0:T(4,128)(2,1)S(1)} %slice.104), channel_id=1, source_target_pairs={{0,4},{1,5},{2,6},{3,7},{4,8},{5,9},{6,10},{7,11},{8,12},{9,13},{1... | collective-permute-start | bytes 18440
  347.9 5.3 copy-start.7
  356.6 245.3 %reduce-scatter.20.cloned.1.call-start = ((), (), s32[]{:S(2)}) async-start(), calls=%async_computation.15 | async-start | bytes 2433024 | tf_op jit(solution)/shard_map/reduce_scatter | solution.py:134
  361.5 6.1 copy-start.22
  361.5 6.1 copy-start.29
  363.8 12.7 %all-to-all-start.2 = ((bf16[384,4,192]{0,2,1:T(8,128)(2,1)}), bf16[384,4,192]{0,2,1:T(8,128)(2,1)S(1)}, u32[]{:S(2)}, u32[]{:S(2)}) async-start(bf16[384,4,192]{0,2,1:T(8,128)(2,1)} %bitcast.40), calls=%async_computation.2 | async-start | bytes 1179648 | tf_op jit(solution)/shard_map/all_to_all | solution.py:227
  367.3 315.8 %reduce-scatter.22.cloned.1.call-start = ((), (), s32[]{:S(2)}) async-start(), calls=%async_computation.16 | async-start | bytes 7299072 | tf_op jit(solution)/shard_map/reduce_scatter | solution.py:136
  372.7 315.3 %reduce-scatter.18.cloned.1.call-start = ((), (), s32[]{:S(2)}) async-start(), calls=%async_computation.14 | async-start | bytes 7299072 | tf_op jit(solution)/shard_map/reduce_scatter | solution.py:133
  591.3 116.3 %reduce-scatter.26.cloned.1.call-start = ((), (), s32[]{:S(2)}) async-start(), calls=%async_computation.19 | async-start | bytes 245760
  597.5 4.3 copy-start.42
  603.6 127.8 %reduce-scatter.28.cloned.1.call-start = ((), (), s32[]{:S(2)}) async-start(), calls=%async_computation.20 | async-start | bytes 737280
  604.9 86.7 %copy-start.10 = (f32[384,768]{1,0:T(8,128)S(1)}, f32[384,768]{1,0:T(8,128)}, u32[]{:S(2)}) copy-start(f32[384,768]{1,0:T(8,128)} %copy-done.9) | copy-start | bytes 3538948
  604.9 86.8 %copy-start.18 = (bf16[1,384,768]{2,1,0:T(8,128)(2,1)S(1)}, bf16[1,384,768]{2,1,0:T(8,128)(2,1)}, u32[]{:S(2)}) copy-start(bf16[1,384,768]{2,1,0:T(8,128)(2,1)} %param.25) | copy-start | bytes 1769476
  686.7 68.6 %reduce-scatter.24.cloned.1.call-start = ((), (), s32[]{:S(2)}) async-start(), calls=%async_computation.18 | async-start | bytes 737280
  (48 other events, 97.6 us)
Sparse Core Ops, SparseCore 0:
  10.3 48.3 all-gather.5
  61.0 42.9 all-gather.11
  106.4 42.2 all-gather.7
  150.8 45.0 all-gather.9
  356.7 23.3 reduce-scatter.29
  384.0 78.6 reduce-scatter.19
  466.4 87.1 reduce-scatter.21
  591.4 94.0 reduce-scatter.17
  687.9 19.6 reduce-scatter.25
  710.0 21.3 reduce-scatter.27
  733.9 21.3 reduce-scatter.23
where the time goes:
time: 777 us; the launch traced here: 764 us
  blocking collectives  260 us (33%)
  matrix products  159 us (20%)
  local copies, waits for them, and re-layouts  149 us (19%)
  waiting for transfers between devices  92.2 us (12%)
  other arithmetic  57.3 us (7%)
  starting transfers between devices  17.4 us (2%)
  between operations  17.2 us (2%)
  loops' own time  11.2 us (1%)
    unnamed x3, blocking collectives  214 us
    dot_general x31, matrix products, times_t(): lax.dot_general(left, right, (((1,), (1,)), ((), ())), preferred_element_...  62.9 us
    unnamed x19, waiting for transfers between devices  61.1 us
    dot_general x22, matrix products, outer_sum(): lax.dot_general(left, right, (((0,), (0,)), ((), ())), preferred_element_...  59.5 us
    all_to_all x1, blocking collectives, body(): lax.all_to_all(stacked_grad, 'seq', split_axis=1, concat_axis=2, tiled=True)  36.9 us
    unnamed x100, local copies, waits for them, and re-layouts  30.9 us
    all_to_all x1, waiting for transfers between devices, body(): lax.all_to_all(stacked, 'seq', split_axis=2, concat_axis=1, tiled=True)  23.6 us
    squeeze x12, local copies, waits for them, and re-layouts, body(): lax.map(run_forward, (head_major[0], head_major[1], head_major[2]))  22.4 us
  transfers between devices with their start and end apart: 18, of which 6 were waited for; matrix products, arithmetic and copies ran while one was open for 44% of the time, Pallas kernels for 0%

commit v1 on v0

v1 whole, which is shorter than its diff:
```python
import math

import jax
import jax.numpy as jnp
from jax import lax
from jax.experimental import pallas as pl
from jax.experimental.pallas import tpu as pltpu
from jax.sharding import PartitionSpec as P

HEADS = 12
HEAD_DIM = 64
LONGEST = 1344
SEQ = 4
LOCAL = 3
TOK = 384
HALF = 192
PACK = 1536
F32 = jnp.float32
BF16 = jnp.bfloat16
VMEM_LIMIT = 60 * 1024 * 1024


def mm(left, right):
    return jnp.dot(left, right, preferred_element_type=F32)


def mm_nt(left, right):
    return lax.dot_general(left, right, (((1,), (1,)), ((), ())), preferred_element_type=F32)


def mm_tn(left, right):
    return lax.dot_general(left, right, (((0,), (0,)), ((), ())), preferred_element_type=F32)


def iota(shape, dim):
    return lax.broadcasted_iota(jnp.int32, shape, dim)


def roll(x, shift):
    return pltpu.roll(x, shift, 1)


def low_lanes(rows):
    return iota((rows, 128), 1) < 64


def turned(x):
    lane = iota(x.shape, 1)
    first = (lane & 32) == 0
    return jnp.where(first, roll(x, 96), roll(x, 32))


def norm_parts(values):
    average = jnp.mean(values, axis=-1, keepdims=True)
    centred = values - average
    variance = jnp.mean(centred * centred, axis=-1, keepdims=True)
    scale = lax.rsqrt(variance + 1e-05)
    return centred * scale, scale


def doc_bounds(len_ref):
    first = len_ref[0]
    second = first + len_ref[1]
    third = second + len_ref[2]
    start = jnp.where(
        len_ref[0] == LONGEST,
        0,
        jnp.where(len_ref[1] == LONGEST, first, jnp.where(len_ref[2] == LONGEST, second, third)),
    )
    return first, second, third, start


def edge_order(start, transposed):
    stored = iota((2 * HALF, 2 * HALF), 1 if transposed else 0)
    edge = iota((2 * HALF, 2 * HALF), 0 if transposed else 1)
    source = stored + (HALF + start)
    source = jnp.where(source >= 2 * HALF, source - 2 * HALF, source)
    return jnp.where(edge == source, 1.0, 0.0).astype(BF16)


def short_mask(bounds):
    first, second, third, start = bounds

    def numbers(dim):
        row = iota((HALF, HALF), dim) + (HALF + start)
        row = jnp.where(row >= 2 * HALF, row - 2 * HALF, row)
        place = jnp.where(row >= HALF, row + (PACK - 2 * HALF), row)
        return (
            jnp.where(place >= first, 1, 0)
            + jnp.where(place >= second, 1, 0)
            + jnp.where(place >= third, 1, 0)
        )

    return numbers(0) == numbers(1)


def extra_lanes(base, column):
    lane = iota(base.shape, 1)
    rest = -column
    top = rest.astype(BF16).astype(F32)
    rest = rest - top
    middle = rest.astype(BF16).astype(F32)
    rest = rest - middle
    return jnp.where(
        lane < 64,
        base,
        jnp.where(lane == 64, top, jnp.where(lane == 65, middle, jnp.where(lane == 66, rest, 0.0))),
    )


def permute_edge(order, ref, head):
    edge = jnp.concatenate([ref[head, 0:HALF, :], ref[head, PACK - HALF : PACK, :]], axis=0)
    moved = mm(order, edge).astype(BF16)
    return moved[0:HALF], moved[HALF : 2 * HALF]


def pack_halves(top, bottom):
    return jnp.where(low_lanes(top.shape[0]), top, roll(bottom, 64))


def project_block(block, hid_ref, w_ref, cos_ref, sin_ref, q_ref, k_ref, v_ref, xt_ref):
    rows = pl.ds(pl.multiple_of(block * TOK, TOK), TOK)
    xhat = norm_parts(hid_ref[block].astype(F32))[0].astype(BF16)
    xt_ref[block] = jnp.transpose(xhat)
    qkv = mm(xhat, w_ref[...])
    cosine, sine = cos_ref[rows, :], sin_ref[rows, :]
    lane = iota((TOK, 128), 1)
    low = lane < 64
    ones = jnp.where(lane < 67, 1.0, 0.0)
    for chunk in range(5):
        part = qkv[:, 128 * chunk : min(128 * chunk + 128, 576)]
        if chunk == 4:
            part = jnp.concatenate([part, part], axis=1)
        if chunk < 3:
            part = part * cosine + turned(part) * sine
        for odd in range(2):
            index = 2 * chunk + odd
            if index == 9:
                continue
            piece = roll(part, 64) if odd else part
            kind, head = index // 3, index % 3
            if kind == 0:
                q_ref[head, rows, :] = (jnp.where(low, piece, 0.0).astype(BF16).astype(F32) * 0.125).astype(BF16)
            elif kind == 1:
                k_ref[head, rows, :] = jnp.where(low, piece, ones).astype(BF16)
            else:
                v_ref[head, rows, :] = jnp.where(low, piece, ones).astype(BF16)


def attend_rows(head, rows, keys, mask, q_ref, k_ref, v_ref, o_ref):
    query = q_ref[head, rows, :]
    scores = mm_nt(query, k_ref[head, keys, :])
    if mask is not None:
        scores = jnp.where(mask, scores, -1e9)
    highest = jnp.max(scores, axis=1, keepdims=True)
    weights = jnp.exp(scores - highest).astype(BF16)
    mixed = mm(weights, v_ref[head, keys, :])
    total = mixed[:, 64:65]
    lane = iota(mixed.shape, 1)
    o_ref[head, rows, :] = jnp.where(lane < 64, mixed * (1.0 / total), 0.0).astype(BF16)
    q_ref[head, rows, :] = extra_lanes(query.astype(F32), highest + jnp.log(total)).astype(BF16)


def forward_kernel(len_ref, hid_ref, w_ref, cos_ref, sin_ref, q_ref, k_ref, v_ref, o_ref, mix_ref, xt_ref):
    bounds = doc_bounds(len_ref)

    @pl.loop(0, SEQ)
    def _(block):
        project_block(block, hid_ref, w_ref, cos_ref, sin_ref, q_ref, k_ref, v_ref, xt_ref)

    order = edge_order(bounds[3], False)
    back = edge_order(bounds[3], True)
    for ref in (q_ref, k_ref, v_ref):
        for head in range(LOCAL):
            short, long = permute_edge(order, ref, head)
            ref[head, 0:HALF, :] = short
            ref[head, PACK - HALF : PACK, :] = long
    mask = short_mask(bounds)
    for head in range(LOCAL):
        attend_rows(head, pl.ds(0, HALF), pl.ds(0, HALF), mask, q_ref, k_ref, v_ref, o_ref)

    @pl.loop(1, PACK // HALF)
    def _(block):
        rows = pl.ds(pl.multiple_of(block * HALF, HALF), HALF)
        for head in range(LOCAL):
            attend_rows(head, rows, pl.ds(HALF, PACK - HALF), None, q_ref, k_ref, v_ref, o_ref)

    for head in range(LOCAL):
        top, bottom = permute_edge(back, o_ref, head)
        for dest in range(SEQ):
            first = top if dest == 0 else o_ref[head, TOK * dest : TOK * dest + HALF, :]
            second = bottom if dest == SEQ - 1 else o_ref[head, TOK * dest + HALF : TOK * dest + TOK, :]
            mix_ref[dest, head] = pack_halves(first.astype(F32), second.astype(F32)).astype(BF16)


def backward_rows(head, rows, queries, mask, q_ref, k_ref, v_ref, d_ref, dk_ref, dv_ref):
    query, grad = q_ref[head, queries, :], d_ref[head, queries, :]
    key = k_ref[head, rows, :]
    shares = jnp.exp(mm_nt(key, query))
    if mask is not None:
        shares = jnp.where(mask, shares, 0.0)
    grad_scores = (shares * mm_nt(v_ref[head, rows, :], grad)).astype(BF16)
    dv_ref[head, rows, :] = mm(shares.astype(BF16), grad).astype(BF16)
    dk_ref[head, rows, :] = mm(grad_scores, query).astype(BF16)
    return mm_tn(grad_scores, key)


def backward_kernel(
    len_ref, g_ref, q_ref, k_ref, v_ref, o_ref, xt_ref, cos_ref, sin_ref,
    out_ref, gw_ref, d_ref, dq_ref, dk_ref, dv_ref, acc_ref, gq_ref,
):
    bounds = doc_bounds(len_ref)
    order = edge_order(bounds[3], False)
    back = edge_order(bounds[3], True)
    low = low_lanes(HALF)
    for head in range(LOCAL):
        for source in range(SEQ):
            packed = g_ref[source, head].astype(F32)
            d_ref[head, TOK * source : TOK * source + HALF, :] = jnp.where(low, packed, 0.0).astype(BF16)
            d_ref[head, TOK * source + HALF : TOK * source + TOK, :] = jnp.where(
                low, roll(packed, 64), 0.0
            ).astype(BF16)
        short, long = permute_edge(order, d_ref, head)
        d_ref[head, 0:HALF, :] = short
        d_ref[head, PACK - HALF : PACK, :] = long

    @pl.loop(0, PACK // HALF)
    def _(block):
        rows = pl.ds(pl.multiple_of(block * HALF, HALF), HALF)
        for head in range(LOCAL):
            grad = d_ref[head, rows, :].astype(F32)
            inner = jnp.sum(grad * o_ref[head, rows, :].astype(F32), axis=1, keepdims=True)
            d_ref[head, rows, :] = extra_lanes(grad, inner).astype(BF16)

    mask = short_mask(bounds)
    for head in range(LOCAL):
        acc_ref[head, 0:HALF, :] = backward_rows(
            head, pl.ds(0, HALF), pl.ds(0, HALF), mask, q_ref, k_ref, v_ref, d_ref, dk_ref, dv_ref
        )
        acc_ref[head, HALF:PACK, :] = jnp.zeros((LONGEST, 128), F32)

    @pl.loop(1, PACK // HALF)
    def _(block):
        rows = pl.ds(pl.multiple_of(block * HALF, HALF), HALF)
        for head in range(LOCAL):
            acc_ref[head, HALF:PACK, :] += backward_rows(
                head, rows, pl.ds(HALF, LONGEST), None, q_ref, k_ref, v_ref, d_ref, dk_ref, dv_ref
            )

    for head in range(LOCAL):
        dq_ref[head] = (acc_ref[head] * 0.125).astype(BF16)
        for ref in (dq_ref, dk_ref, dv_ref):
            top, bottom = permute_edge(back, ref, head)
            ref[head, 0:HALF, :] = top
            ref[head, PACK - HALF : PACK, :] = bottom

    @pl.loop(0, SEQ)
    def _(dest):
        top = pl.ds(pl.multiple_of(dest * TOK, TOK), HALF)
        bottom = pl.ds(pl.multiple_of(dest * TOK + HALF, HALF), HALF)
        cosine = pack_halves(cos_ref[top, :], cos_ref[bottom, :])
        sine = pack_halves(sin_ref[top, :], sin_ref[bottom, :])
        blocks = []
        for kind, ref in enumerate((dq_ref, dk_ref, dv_ref)):
            for head in range(LOCAL):
                packed = pack_halves(ref[head, top, :].astype(F32), ref[head, bottom, :].astype(F32))
                if kind < 2:
                    packed = packed * cosine - turned(packed) * sine
                out_ref[dest, head, kind] = packed.astype(BF16)
                blocks.append(packed)
        for chunk in range(5):
            one = blocks[2 * chunk]
            two = blocks[2 * chunk + 1] if chunk < 4 else jnp.zeros_like(one)
            gq_ref[top, 128 * chunk : 128 * chunk + 128] = pack_halves(one, two).astype(BF16)
            gq_ref[bottom, 128 * chunk : 128 * chunk + 128] = jnp.where(low, roll(one, 64), two).astype(BF16)

    total = mm(xt_ref[0], gq_ref[0:TOK, :])
    for block in range(1, SEQ):
        total += mm(xt_ref[block], gq_ref[TOK * block : TOK * block + TOK, :])
    gw_ref[...] = total[:, :576].astype(BF16)


def middle_kernel(
    hid_ref, mix_ref, wo_ref, wi_ref, wd_ref, cot_ref,
    out_ref, gres_ref, gmix_ref, go_ref, gi_ref, gd_ref,
    attn_ref, x_ref, proj_ref, act_ref, gp_ref,
):
    low = low_lanes(HALF)
    for chunk in range(6):
        pair = []
        for index in (2 * chunk, 2 * chunk + 1):
            pair.append(mix_ref[index // 3, index % 3].astype(F32))
        one, two = pair
        lanes = slice(128 * chunk, 128 * chunk + 128)
        attn_ref[0:HALF, lanes] = pack_halves(one, two).astype(BF16)
        attn_ref[HALF:TOK, lanes] = jnp.where(low, roll(one, 64), two).astype(BF16)
    residual = hid_ref[...].astype(F32) + mm(attn_ref[...], wo_ref[...])
    xhat, scale = norm_parts(residual)
    x_ref[...] = xhat.astype(BF16)
    ff = wd_ref.shape[0]
    step = 384
    for chunk in range(2 * ff // step):
        lanes = slice(step * chunk, step * chunk + step)
        proj_ref[:, lanes] = mm(x_ref[...], wi_ref[:, lanes])
    output = residual
    branch = cot_ref[...]
    for chunk in range(ff // step):
        lanes = slice(step * chunk, step * chunk + step)
        inner = proj_ref[:, lanes]
        gate = proj_ref[:, ff + step * chunk : ff + step * chunk + step]
        phi = 0.5 * (1.0 + lax.erf(inner * math.sqrt(0.5)))
        gelu = inner * phi
        act = (gelu * gate).astype(BF16)
        act_ref[:, lanes] = act
        output = output + mm(act, wd_ref[lanes, :])
        grad_act = mm_nt(branch, wd_ref[lanes, :])
        density = jnp.exp(inner * inner * -0.5) * (1.0 / math.sqrt(2.0 * math.pi))
        gp_ref[:, lanes] = (grad_act * gate * (phi + inner * density)).astype(BF16)
        gp_ref[:, ff + step * chunk : ff + step * chunk + step] = (grad_act * gelu).astype(BF16)
    out_ref[...] = output.astype(BF16)
    grad = mm_nt(gp_ref[...], wi_ref[...])
    grad = scale * (
        grad
        - jnp.mean(grad, axis=-1, keepdims=True)
        - xhat * jnp.mean(grad * xhat, axis=-1, keepdims=True)
    )
    grad_res = branch.astype(F32) + grad
    gres_ref[...] = grad_res
    grad_attn = grad_res.astype(BF16)
    grad_mix = mm_nt(grad_attn, wo_ref[...]).astype(BF16).astype(F32)
    for chunk in range(6):
        lanes = slice(128 * chunk, 128 * chunk + 128)
        top, bottom = grad_mix[0:HALF, lanes], grad_mix[HALF:TOK, lanes]
        one = pack_halves(top, bottom)
        two = jnp.where(low, roll(top, 64), bottom)
        gmix_ref[2 * chunk // 3, 2 * chunk % 3] = one.astype(BF16)
        gmix_ref[(2 * chunk + 1) // 3, (2 * chunk + 1) % 3] = two.astype(BF16)
    go_ref[...] = mm_tn(attn_ref[...], grad_attn).astype(BF16)
    for chunk in range(2 * ff // step):
        lanes = slice(step * chunk, step * chunk + step)
        gi_ref[:, lanes] = mm_tn(x_ref[...], gp_ref[:, lanes]).astype(BF16)
    for chunk in range(ff // step):
        lanes = slice(step * chunk, step * chunk + step)
        gd_ref[lanes, :] = mm_tn(act_ref[:, lanes], branch).astype(BF16)


def last_kernel(g_ref, w_ref, hid_ref, gres_ref, out_ref, full_ref):
    low = low_lanes(HALF)
    for chunk in range(18):
        pair = []
        for index in (2 * chunk, 2 * chunk + 1):
            kind, head = index // HEADS, index % HEADS
            pair.append(g_ref[head // 3, head % 3, kind].astype(F32))
        one, two = pair
        lanes = slice(128 * chunk, 128 * chunk + 128)
        full_ref[0:HALF, lanes] = pack_halves(one, two).astype(BF16)
        full_ref[HALF:TOK, lanes] = jnp.where(low, roll(one, 64), two).astype(BF16)
    grad = mm_nt(full_ref[...], w_ref[...])
    xhat, scale = norm_parts(hid_ref[...].astype(F32))
    grad = scale * (
        grad
        - jnp.mean(grad, axis=-1, keepdims=True)
        - xhat * jnp.mean(grad * xhat, axis=-1, keepdims=True)
    )
    out_ref[...] = gres_ref[...] + grad


SMEM = pl.BlockSpec(memory_space=pltpu.SMEM)
VMEM = pl.BlockSpec(memory_space=pltpu.VMEM)


def shape(*dims, dtype=BF16):
    return jax.ShapeDtypeStruct(dims, dtype)


def call(kernel, args, outs, scratch=(), smem=False):
    specs = [VMEM] * len(args)
    if smem:
        specs[0] = SMEM
    return pl.pallas_call(
        kernel,
        out_shape=outs,
        in_specs=specs,
        out_specs=jax.tree.map(lambda _: VMEM, outs),
        scratch_shapes=list(scratch),
        compiler_params=pltpu.CompilerParams(vmem_limit_bytes=VMEM_LIMIT),
    )(*args)


def rope_tables(lengths):
    ends = jnp.cumsum(lengths)
    places = jnp.arange(PACK, dtype=jnp.int32)
    started = jnp.where(places[:, None] >= ends[None, :3], lengths[None, :3], 0)
    position = (places - jnp.sum(started, axis=1)).astype(F32)
    lane = jnp.arange(128, dtype=jnp.int32)
    inverse = jnp.exp((lane % 32).astype(F32) * (-2.0 * math.log(160000.0) / HEAD_DIM))
    angles = position[:, None] * inverse[None, :]
    sign = jnp.where((lane & 32) == 0, -1.0, 1.0)
    return jnp.cos(angles), jnp.sin(angles) * sign


def body(hidden, lengths, attn_gain, w_qkv, w_attn_out, mlp_gain, w_in, w_mlp_out, cotangent):
    rank = lax.axis_index("seq")
    lengths = lengths[0]
    gain_one = attn_gain.astype(F32)[:, None]
    gain_two = mlp_gain.astype(F32)[:, None]
    w_one = (w_qkv.astype(F32) * gain_one).astype(BF16)
    w_two = (w_in.astype(F32) * gain_two).astype(BF16)
    own = lax.dynamic_index_in_dim(w_one.reshape(-1, 3, SEQ, 192), rank, 2, keepdims=False).reshape(-1, 576)

    def gather(x):
        return lax.all_gather(x, "fsdp", axis=0, tiled=True)

    own_full, one_full, out_full = gather(own), gather(w_one), gather(w_attn_out)
    two_full, down_full = gather(w_two), gather(w_mlp_out)
    hidden_full = lax.all_gather(hidden[0], "seq", axis=0)
    cosine, sine = rope_tables(lengths)
    head_shape = shape(LOCAL, PACK, 128)
    q, k, v, o, mix, xt = call(
        forward_kernel,
        (lengths, hidden_full, own_full, cosine, sine),
        (head_shape, head_shape, head_shape, head_shape, shape(SEQ, LOCAL, HALF, 128), shape(SEQ, 768, TOK)),
        smem=True,
    )
    mix = lax.all_to_all(mix, "seq", 0, 0)
    ff = down_full.shape[0]
    output, grad_res, grad_mix, grad_out, grad_in, grad_down = call(
        middle_kernel,
        (hidden[0], mix, out_full, two_full, down_full, cotangent[0]),
        (
            shape(TOK, 768),
            shape(TOK, 768, dtype=F32),
            shape(SEQ, LOCAL, HALF, 128),
            shape(768, 768),
            shape(768, 2 * ff),
            shape(ff, 768),
        ),
        (
            pltpu.VMEM((TOK, 768), BF16),
            pltpu.VMEM((TOK, 768), BF16),
            pltpu.VMEM((TOK, 2 * ff), F32),
            pltpu.VMEM((TOK, ff), BF16),
            pltpu.VMEM((TOK, 2 * ff), BF16),
        ),
    )
    grad_mix = lax.all_to_all(grad_mix, "seq", 0, 0)
    grads, grad_own = call(
        backward_kernel,
        (lengths, grad_mix, q, k, v, o, xt, cosine, sine),
        (shape(SEQ, LOCAL, 3, HALF, 128), shape(768, 576)),
        (
            pltpu.VMEM((LOCAL, PACK, 128), BF16),
            pltpu.VMEM((LOCAL, PACK, 128), BF16),
            pltpu.VMEM((LOCAL, PACK, 128), BF16),
            pltpu.VMEM((LOCAL, PACK, 128), BF16),
            pltpu.VMEM((LOCAL, PACK, 128), F32),
            pltpu.VMEM((PACK, 640), BF16),
        ),
        smem=True,
    )
    grads = lax.all_to_all(grads, "seq", 0, 0)
    input_grad = call(
        last_kernel,
        (grads, one_full, hidden[0], grad_res),
        shape(TOK, 768, dtype=F32),
        (pltpu.VMEM((TOK, 2304), BF16),),
    )

    def scatter(x):
        return lax.psum_scatter(x, "fsdp", scatter_dimension=0, tiled=True)

    def columns(x):
        return lax.psum_scatter(x, "seq", scatter_dimension=1, tiled=True).astype(F32)

    rows_in = scatter(grad_in)
    rows_own = scatter(grad_own).astype(F32)
    gain_part_two = jnp.sum(rows_in.astype(F32) * w_in.astype(F32), axis=1)
    own_raw = lax.dynamic_index_in_dim(w_qkv.reshape(-1, 3, SEQ, 192), rank, 2, keepdims=False).reshape(-1, 576)
    gain_part_one = jnp.sum(rows_own * own_raw.astype(F32), axis=1)
    grad_gain_one, grad_gain_two = lax.psum((gain_part_one, gain_part_two), "seq")
    spread = lax.all_gather((rows_own * gain_one).reshape(-1, 3, 192), "seq", axis=2)
    grad_qkv = lax.dynamic_slice_in_dim(spread.reshape(-1, 2304), rank * 576, 576, axis=1)
    return (
        output[None],
        input_grad[None],
        grad_gain_one,
        grad_qkv,
        columns(scatter(grad_out)),
        grad_gain_two,
        columns(rows_in) * gain_two,
        columns(scatter(grad_down)),
    )


def solution(mesh):
    in_specs = (
        P("fsdp", "seq", None),
        P("fsdp", None),
        P("fsdp"),
        P("fsdp", None),
        P("fsdp", None),
        P("fsdp"),
        P("fsdp", None),
        P("fsdp", None),
        P("fsdp", "seq", None),
    )
    out_specs = (
        P("fsdp", "seq", None),
        P("fsdp", "seq", None),
        P("fsdp"),
        P("fsdp", "seq"),
        P("fsdp", "seq"),
        P("fsdp"),
        P("fsdp", "seq"),
        P("fsdp", "seq"),
    )
    return jax.shard_map(body, mesh=mesh, in_specs=in_specs, out_specs=out_specs, check_vma=False)
```

time: 777 us -> 667 us (0.86); the launches traced: 764 us -> 666 us
  waiting for transfers between devices: 92.2 us -> 397 us
  matrix products: 159 us -> 0 us
  blocking collectives: 260 us -> 128 us
  local copies, waits for them, and re-layouts: 149 us -> 17.1 us
  Pallas kernels: 0 us -> 77.2 us
  other arithmetic: 57.3 us -> 12.5 us
  loops' own time: 11.2 us -> 0 us
    dot_general x75 -> x0, matrix products: 159 us -> none  [the longest x31 62.9 us: times_t(): lax.dot_general(left, right, (((1,), (1,)), ((), ())), preferred_element_...]
    reduce_scatter x3 -> x2, waiting for transfers between devices: 0.02 us -> 154 us  [scatter(): return lax.psum_scatter(x, 'fsdp', scatter_dimension=0, tiled=True)]
    unnamed x3 -> x1, blocking collectives: 214 us -> 77 us
    all_gather x4 -> x5, waiting for transfers between devices: 0.05 us -> 137 us  [the longest x4 137 us: gather(): return lax.all_gather(x, 'fsdp', axis=0, tiled=True)]
    pallas_call x0 -> x4, Pallas kernels: none -> 77.2 us  [call(): pl.pallas_call(kernel, out_shape=outs, in_specs=specs, out_specs=jax.tree...]
    unnamed x19, waiting for transfers between devices: 61.1 us -> 107 us
    all_gather x0 -> x2, blocking collectives: none -> 41.5 us  [the longest x1 28.8 us: gather(): return lax.all_gather(x, 'fsdp', axis=0, tiled=True)]
    all_to_all x1 -> x0, blocking collectives: 36.9 us -> none  [body(): lax.all_to_all(stacked_grad, 'seq', split_axis=1, concat_axis=2, tiled=True)]
  transfers between devices with their start and end apart: 18 -> 18, of which waited for: 6 -> 10; matrix products, arithmetic and copies ran while one was open for 44% -> 15% of each run, Pallas kernels for 0% -> 9%
where the time goes in v1:
time: 667 us; the launch traced here: 666 us
  waiting for transfers between devices  397 us (60%)
  blocking collectives  128 us (19%)
  Pallas kernels  77.2 us (12%)
  starting transfers between devices  19 us (3%)
  local copies, waits for them, and re-layouts  17.1 us (3%)
  between operations  14.7 us (2%)
  other arithmetic  12.5 us (2%)
    reduce_scatter x2, waiting for transfers between devices, scatter(): return lax.psum_scatter(x, 'fsdp', scatter_dimension=0, tiled=True)  154 us
    all_gather x4, waiting for transfers between devices, gather(): return lax.all_gather(x, 'fsdp', axis=0, tiled=True)  137 us
    unnamed x19, waiting for transfers between devices  107 us
    pallas_call x4, Pallas kernels, call(): pl.pallas_call(kernel, out_shape=outs, in_specs=specs, out_specs=jax.tree...  77.2 us
    unnamed x1, blocking collectives  77 us
    all_gather x1, blocking collectives, gather(): return lax.all_gather(x, 'fsdp', axis=0, tiled=True)  28.8 us
    unnamed x25, local copies, waits for them, and re-layouts  14.2 us
  transfers between devices with their start and end apart: 18, of which 10 were waited for; matrix products, arithmetic and copies ran while one was open for 15% of the time, Pallas kernels for 9%

profile of v1, /device:TPU:0, one launch (start us, length us, event | category | flops | bytes accessed | tf_op | source)
XLA Modules:
  0.0 665.5 jit_solution(2038656554831803070)
XLA Ops:
  10.1 1.6 fusion.2
  12.4 1.1 reshape.73
  15.4 28.8 %all_gather.22.w_ref = bf16[768,576]{1,0:T(8,128)(2,1)} all-gather(bf16[24,576]{1,0:T(8,128)(2,1)S(1)} %reshape.71), channel_id=1, replica_groups=mesh['seq'=4,'fsdp'=32] {'fsdp'}, dimensions={0}, use_global_device_ids=true | all-gather | bytes 912384 | tf_op jit(solution)/shard_map/all_gather | solution.py:412
  44.2 4.3 fusion.1
  48.5 22.9 %shard_map.152 = (bf16[3,1536,128]{2,1,0:T(8,128)(2,1)}, bf16[3,1536,128]{2,1,0:T(8,128)(2,1)}, bf16[3,1536,128]{2,1,0:T(8,128)(2,1)}, bf16[3,1536,128]{2,1,0:T(...) custom-call(s32[4]{0:T(128)} %bitcast.33, ...), custom_call_target="tpu_custom_call" | custom-call | tf_op jit(solution)/shard_map/pallas_call | solution.py:380
  71.4 4.3 all-to-all-start
  75.7 15.7 %all-gather.15.cloned.1.call-done = bf16[32,36,768]{2,1,0:T(8,128)(2,1)} async-done(((bf16[1,36,768]{2,1,0:T(8,128)(2,1)}), bf16[32,36,768]{2,1,0:T(8,128)(2,1)}) %all-gather.15.cloned.1.call-update) | async-done | bytes 1769488 | tf_op jit(solution)/shard_map/all_gather | solution.py:412
  91.4 3.6 reshape.77.wd_ref
  95.0 41.0 %all-gather.9.cloned.1.call-done.wo_ref = bf16[768,768]{1,0:T(8,128)(2,1)} async-done(((bf16[24,768]{1,0:T(8,128)(2,1)}), bf16[768,768]{1,0:T(8,128)(2,1)}) %all-gather.9.cloned.1.call-update) | async-done | bytes 1179664 | tf_op jit(solution)/shard_map/all_gather | solution.py:412
  136.0 47.2 %all-gather.11.cloned.1.call-done.wi_ref = bf16[768,2304]{1,0:T(8,128)(2,1)} async-done(((bf16[24,2304]{1,0:T(8,128)(2,1)}), bf16[768,2304]{1,0:T(8,128)(2,1)}) %all-gather.11.cloned.1.call-update) | async-done | bytes 3538960 | tf_op jit(solution)/shard_map/all_gather | solution.py:412
  183.2 16.3 %shard_map.153 = (bf16[384,768]{1,0:T(8,128)(2,1)}, f32[384,768]{1,0:T(8,128)}, bf16[4,3,192,128]{3,2,1,0:T(8,128)(2,1)}, bf16[768,768]{1,0:T(8,128)(2,1)}, bf16...) custom-call(bf16[384,768]{1,0:T(8,128)(2,1)} %bitcast.22, bf16[4,3,192,128]{3,2,1,0:T(8,128)(2,1)} %copy-done.2, ...), custom_call_target="tpu_custom_call" | custom-call | tf_op jit(solution)/shard_map/pallas_call | solution.py:380
  199.5 4.4 all-to-all-start.1
  203.9 77.0 %fusion = bf16[40,768]{1,0:T(8,128)(2,1)S(1)} fusion(bf16[1152,768]{1,0:T(8,128)(2,1)} %get-tuple-element.35), kind=kCustom, calls=%all-reduce-scatter | all-reduce-scatter fusion | flops 983041 | bytes 1831424
  280.9 1.3 collective-permute-start
  282.2 1.3 collective-permute-start.1
  283.5 1.3 collective-permute-start.2
  284.8 1.3 collective-permute-start.3
  290.2 31.7 %shard_map.154 = (bf16[4,3,3,192,128]{4,3,2,1,0:T(8,128)(2,1)}, bf16[768,576]{1,0:T(8,128)(2,1)}) custom-call(s32[4]{0:T(128)} %bitcast.34, bf16[4,3,192,128]{3,2,1,0:T(8,128)(2,1)} %copy-done.1, bf16[3,1536,128]{2,1,0:T(8,128)(2,1)} %get-tuple-element.25.q_ref, bf16[3,1536,128]{2,1,0:T(8,128)(2,1)} %get-tuple-element.26.k_ref, ...), custom_call_target="tpu_custom_call" | custom-call | tf_op jit(solution)/shard_map/pallas_call | solution.py:380
  324.2 4.5 all-to-all-start.2
  330.3 71.2 %reduce-scatter.27.cloned.1.call-done = bf16[24,576]{1,0:T(8,128)(2,1)} async-done(((bf16[768,576]{1,0:T(8,128)(2,1)}), bf16[24,576]{1,0:T(8,128)(2,1)}) %reduce-scatter.27.cloned.1.call-update) | async-done | bytes 27664
  402.6 77.8 %reduce-scatter.17.cloned.1.call-done = bf16[24,768]{1,0:T(8,128)(2,1)} async-done(((bf16[768,768]{1,0:T(8,128)(2,1)}), bf16[24,768]{1,0:T(8,128)(2,1)}) %reduce-scatter.17.cloned.1.call-update) | async-done | bytes 36880 | tf_op jit(solution)/shard_map/reduce_scatter | solution.py:470
  480.5 1.6 copy.32
  482.1 12.7 %all_gather.27 = f32[24,3,4,192]{3,0,1,2:T(8,128)S(1)} all-gather(f32[24,3,1,192]{3,0,1,2:T(8,128)S(1)} %copy.30), channel_id=1, replica_groups=mesh['seq'=4,'fsdp'=32] {'seq'}, dimensions={2}, use_global_device_ids=true | all-gather | bytes 276480 | tf_op jit(solution)/shard_map/all_gather | solution.py:481
  495.2 32.7 %all-gather.13.cloned.1.call-done.w_ref = bf16[768,2304]{1,0:T(8,128)(2,1)} async-done(((bf16[24,2304]{1,0:T(8,128)(2,1)}), bf16[768,2304]{1,0:T(8,128)(2,1)}) %all-gather.13.cloned.1.call-update) | async-done | bytes 3538960 | tf_op jit(solution)/shard_map/all_gather | solution.py:412
  527.9 1.2 copy-done
  529.1 6.4 shard_map.155
  535.4 76.0 %reduce-scatter.19.cloned.1.call-done = bf16[24,2304]{1,0:T(8,128)(2,1)} async-done(((bf16[768,2304]{1,0:T(8,128)(2,1)}), bf16[24,2304]{1,0:T(8,128)(2,1)}) %reduce-scatter.19.cloned.1.call-update) | async-done | bytes 110608 | tf_op jit(solution)/shard_map/reduce_scatter | solution.py:470
  611.4 2.0 copy.34
  614.1 19.2 %reduce-scatter.21.cloned.1.call-done = bf16[192,24]{1,0:T(8,128)(2,1)} async-done(((bf16[768,24]{1,0:T(8,128)(2,1)}), bf16[192,24]{1,0:T(8,128)(2,1)}) %reduce-scatter.21.cloned.1.call-update) | async-done | bytes 9232
  634.8 1.0 fusion.3
  635.9 9.1 %all-reduce.3 = (f32[24]{0:T(128)}, f32[24]{0:T(128)}) all-reduce(f32[24]{0:T(128)S(1)} %get-tuple-element.39, f32[24]{0:T(128)S(1)} %fusion.3), channel_id=1, replica_groups=mesh['seq'=4,'fsdp'=32] {'seq'}, use_global_device_ids=true, to_apply=%region_4.5 | all-reduce | flops 48 | bytes 384 | tf_op jit(solution)/shard_map/psum | solution.py:480
  644.9 12.4 %reduce-scatter.23.cloned.1.call-done = bf16[576,24]{1,0:T(8,128)(2,1)} async-done(((bf16[2304,24]{1,0:T(8,128)(2,1)}), bf16[576,24]{1,0:T(8,128)(2,1)}) %reduce-scatter.23.cloned.1.call-update) | async-done | bytes 27664
  (75 shorter events, 18.0 us)
Async XLA Ops:
  7.2 7.9 %copy-start.5 = (s32[1,4]{1,0:T(1,128)S(1)}, s32[1,4]{1,0:T(1,128)}, u32[]{:S(2)}) copy-start(s32[1,4]{1,0:T(1,128)} %param.10) | copy-start | bytes 52
  7.2 41.3 %all-gather.7.cloned.1.call-start = ((), (), s32[]{:S(2)}) async-start(), calls=%async_computation.9 | async-start | bytes 2949120 | tf_op jit(solution)/shard_map/all_gather | solution.py:416
  7.9 83.5 %all-gather.15.cloned.1.call-start = ((), (), s32[]{:S(2)}) async-start(), calls=%async_computation.15 | async-start | bytes 2027520 | tf_op jit(solution)/shard_map/all_gather | solution.py:412
  8.7 127.3 %all-gather.9.cloned.1.call-start = ((), (), s32[]{:S(2)}) async-start(), calls=%async_computation.10 | async-start | bytes 1216512 | tf_op jit(solution)/shard_map/all_gather | solution.py:412
  9.4 173.8 %all-gather.11.cloned.1.call-start = ((), (), s32[]{:S(2)}) async-start(), calls=%async_computation.11 | async-start | bytes 3649536 | tf_op jit(solution)/shard_map/all_gather | solution.py:412
  14.5 56.9 %copy-start.3 = (bf16[24,2304]{1,0:T(8,128)(2,1)}, bf16[24,2304]{1,0:T(8,128)(2,1)S(1)}, u32[]{:S(2)}) copy-start(bf16[24,2304]{1,0:T(8,128)(2,1)S(1)} %multiply_convert_fusion) | copy-start | bytes 331780
  71.4 64.6 %all-to-all-start = ((bf16[4,3,192,128]{3,2,1,0:T(8,128)(2,1)}), bf16[4,3,192,128]{3,2,1,0:T(8,128)(2,1)S(1)}, u32[]{:S(2)}, u32[]{:S(2)}) async-start(bf16[4,3,192,128]{3,2,1,0:T(8,128)(2,1)} %get-tuple-element.22), calls=%async_computation | async-start | bytes 1179648 | tf_op jit(solution)/shard_map/all_to_all | solution.py:425
  136.0 47.3 %copy-start.2 = (bf16[4,3,192,128]{3,2,1,0:T(8,128)(2,1)}, bf16[4,3,192,128]{3,2,1,0:T(8,128)(2,1)S(1)}, u32[]{:S(2)}) copy-start(bf16[4,3,192,128]{3,2,1,0:T(8,128)(2,1)S(1)} %all-to-all-done.mix_ref) | copy-start | bytes 1769476
  199.5 86.6 %copy-start.6 = (u32[128]{0:T(128)S(1)}, u32[128]{0:T(128)}, u32[]{:S(2)}) copy-start(u32[128]{0:T(128)} %constant.58) | copy-start | bytes 1540
  199.5 89.8 %all-to-all-start.1 = ((bf16[4,3,192,128]{3,2,1,0:T(8,128)(2,1)}), bf16[4,3,192,128]{3,2,1,0:T(8,128)(2,1)S(1)}, u32[]{:S(2)}, u32[]{:S(2)}) async-start(bf16[4,3,192,128]{3,2,1,0:T(8,128)(2,1)} %get-tuple-element.24), calls=%async_computation.1 | async-start | bytes 1179648 | tf_op jit(solution)/shard_map/all_to_all | solution.py:446
  203.9 124.9 %reduce-scatter.25.cloned.1.call-start = ((), (), s32[]{:S(2)}) async-start(), calls=%async_computation.18 | async-start | bytes 245760
  280.9 6.5 collective-permute-start
  282.2 5.3 collective-permute-start.1
  283.5 4.0 collective-permute-start.2
  284.8 2.6 collective-permute-start.3
  289.1 112.5 %reduce-scatter.27.cloned.1.call-start = ((), (), s32[]{:S(2)}) async-start(), calls=%async_computation.19 | async-start | bytes 1013760
  289.3 0.8 copy-start.1
  321.9 158.5 %reduce-scatter.17.cloned.1.call-start = ((), (), s32[]{:S(2)}) async-start(), calls=%async_computation.13 | async-start | bytes 1216512 | tf_op jit(solution)/shard_map/reduce_scatter | solution.py:470
  322.7 205.2 %all-gather.13.cloned.1.call-start = ((), (), s32[]{:S(2)}) async-start(), calls=%async_computation.12 | async-start | bytes 3649536 | tf_op jit(solution)/shard_map/all_gather | solution.py:412
  323.4 288.0 %reduce-scatter.19.cloned.1.call-start = ((), (), s32[]{:S(2)}) async-start(), calls=%async_computation.14 | async-start | bytes 3649536 | tf_op jit(solution)/shard_map/reduce_scatter | solution.py:470
  324.2 203.7 %all-to-all-start.2 = ((bf16[4,3,3,192,128]{4,3,2,1,0:T(8,128)(2,1)}), bf16[4,3,3,192,128]{4,3,2,1,0:T(8,128)(2,1)S(1)}, u32[]{:S(2)}, u32[]{:S(2)}) async-start(bf16[4,3,3,192,128]{4,3,2,1,0:T(8,128)(2,1)} %get-tuple-element.30), calls=%async_computation.2 | async-start | bytes 3538944 | tf_op jit(solution)/shard_map/all_to_all | solution.py:461
  328.7 304.6 %reduce-scatter.21.cloned.1.call-start = ((), (), s32[]{:S(2)}) async-start(), calls=%async_computation.16 | async-start | bytes 245760
  482.1 175.2 %reduce-scatter.23.cloned.1.call-start = ((), (), s32[]{:S(2)}) async-start(), calls=%async_computation.17 | async-start | bytes 737280
  527.9 1.2 copy-start
  529.1 105.7 %copy-start.4 = (bf16[24,2304]{1,0:T(8,128)(2,1)S(1)}, bf16[24,2304]{1,0:T(8,128)(2,1)}, u32[]{:S(2)}) copy-start(bf16[24,2304]{1,0:T(8,128)(2,1)} %param.15) | copy-start | bytes 331780
Sparse Core Ops, SparseCore 0:
  9.7 35.4 all-gather.6
  47.5 43.8 all-gather.14
  93.7 42.2 all-gather.8
  138.2 45.0 all-gather.10
  289.2 23.9 reduce-scatter.24
  322.0 79.4 reduce-scatter.26
  405.1 75.2 reduce-scatter.16
  482.8 45.0 all-gather.12
  531.6 79.7 reduce-scatter.18
  613.6 19.6 reduce-scatter.20
  635.9 21.3 reduce-scatter.22
